TPU v7x, 256 devices: a whole 4x4x8 slice. The times are simulated.
256 devices in a mesh: rep: 32 (over z_lo, y, core), fsdp: 8 (over z_hi, x).
Axes of the slice: x: 4, y: 4, z: 8 (z_hi: 2, z_lo: 4; z = z_hi * 4 + z_lo), core: 2. Of those that a mesh axis runs over, the one named last changes fastest.
Arguments:
- params: bfloat16 [32, 7168, 2048], P('rep', 'fsdp'), may hold values from -6 to 6
- hidden_acts: bfloat16 [32, 1024, 7168], P('rep', 'fsdp'), may hold values from -6 to 6
- out_grads: bfloat16 [32, 1024, 2048], P('rep', 'fsdp'), may hold values from -6 to 6
- step_counts: int32 [32], P('rep'), may hold values from 1 to 32
- outer_z: float32 [7168, 2048], P('fsdp', 'rep'), may hold values from -4 to 4
- outer_x: float32 [7168, 2048], P('fsdp', 'rep'), may hold values from -4 to 4
Outputs:
- new_z: float32 [7168, 2048], P('fsdp', 'rep')
- new_x: float32 [7168, 2048], P('fsdp', 'rep')
- new_y: bfloat16 [7168, 2048], P('fsdp')
All inputs are finite; a program needn't handle non-finite values.
Results may differ from a plain program's by a relative error of at most 0.0055.
Values may be sent and summed in bfloat16 or wider, within the bound.
A program may use at most 128 MiB of HBM per device.

v0:
```python
import jax
import jax.numpy as jnp
from jax import lax
from jax.sharding import Mesh
from jax.sharding import PartitionSpec as P

ROUND = 3
FSDP = ("fsdp_0", "fsdp_1")


def in_order(parts, dim):
    shape = list(parts.shape[1:])
    shape[dim] *= parts.shape[0]
    return jnp.moveaxis(parts, 0, dim).reshape(shape)


def all_blocks(array, axes, sequence):
    parts = array
    for k in sequence:
        parts = lax.all_gather(parts, axes[k])
    done = sequence[::-1]
    back = [done.index(k) for k in range(len(axes))]
    parts = parts.transpose(*back, *range(len(axes), parts.ndim))
    return parts.reshape(-1, *array.shape)


def gathered_by_axis(array, axes, sequence, dim):
    return in_order(all_blocks(array, axes, sequence), dim)


def sent_to_all(array, axis):
    copies = jnp.broadcast_to(array, (lax.axis_size(axis), *array.shape))
    return lax.all_to_all(copies, axis, split_axis=0, concat_axis=0, tiled=True)


def collect(array, axis, dim):
    parts = sent_to_all(array, axis)
    return in_order(parts, dim)


def transposed_product(left, right):
    return lax.dot_general(
        left, right, (((0,), (0,)), ((), ())), preferred_element_type=jnp.float32
    )


def local(params, hidden_acts, out_grads, step_counts, outer_z, outer_x):
    rows = params.shape[1]
    hidden_cols = lax.all_to_all(hidden_acts[0], FSDP, split_axis=1, concat_axis=0, tiled=True)
    grad = transposed_product(hidden_cols, gathered_by_axis(out_grads[0], FSDP, (0, 1), 0))
    inner = (params[0].astype(jnp.float32) - 0.1 * grad).astype(jnp.bfloat16)
    every_count = collect(step_counts, "rep", 0)
    replicas = every_count.shape[0]
    blocks = lax.all_to_all(inner, "rep", split_axis=1, concat_axis=0, tiled=True)
    columns = blocks.shape[1]
    stacked = blocks.reshape(replicas, rows * columns)
    weights = every_count.astype(jnp.bfloat16).reshape(1, replicas)
    summed = jnp.dot(weights, stacked, preferred_element_type=jnp.float32).reshape(rows, columns)
    total_f = jnp.sum(every_count).astype(jnp.float32)
    anchor = 0.1 * outer_z + 0.9 * outer_x
    pseudo = anchor - summed / total_f
    new_z = outer_z - 0.7 * pseudo
    mixing = 1.0 / (ROUND + 1.0)
    new_x = (1.0 - mixing) * outer_x + mixing * new_z
    block_y = (0.1 * new_z + 0.9 * new_x).astype(jnp.bfloat16)
    new_y = lax.all_gather(block_y, "rep", axis=1, tiled=True)
    return (new_z, new_x, new_y)


def solution(mesh):
    split = Mesh(mesh.devices.reshape(mesh.shape["rep"], 2, 4), ("rep", "fsdp_0", "fsdp_1"))
    placed = (
        P("rep", FSDP, None),
        P("rep", FSDP, None),
        P("rep", FSDP, None),
        P("rep"),
        P(FSDP, "rep"),
        P(FSDP, "rep"),
    )
    return jax.shard_map(
        local,
        mesh=split,
        in_specs=placed,
        out_specs=(P(FSDP, "rep"), P(FSDP, "rep"), P(FSDP, None)),
        check_vma=False,
    )
```

profile of v0, /device:TPU:1, one launch (start us, length us, event | category | flops | bytes accessed | tf_op | source)
XLA Modules:
  0.0 332.2 jit_solution(4786897905896339161)
XLA Ops:
  7.2 0.0 all-gather.5.cloned.1.call-start
  7.2 0.7 all-gather.5.cloned.1.call-update
  7.9 0.0 all-gather.9.cloned.1.call-start
  7.9 47.6 %all-gather.5.cloned.1.call-done = bf16[2,128,2048]{2,1,0:T(8,128)(2,1)} async-done(((bf16[1,128,2048]{2,1,0:T(8,128)(2,1)}), bf16[2,128,2048]{2,1,0:T(8,128)(2,1)}) %all-gather.5.cloned.1.call-update) | async-done | bytes 1048592 | tf_op jit(solution)/shard_map/all_gather | solution.py:20
  55.6 0.0 all-gather.9.cloned.1.call-update
  55.6 3.9 %copy.40 = bf16[1,128,7168]{1,2,0:T(8,128)(2,1)} copy(bf16[1,128,7168]{2,1,0:T(8,128)(2,1)} %param.7) | data formatting | bytes 3670016 | tf_op args[1]
  59.5 4.0 %all-to-all-start = ((bf16[128,8,896]{0,2,1:T(8,128)(2,1)}), bf16[128,8,896]{0,2,1:T(8,128)(2,1)S(1)}, u32[]{:S(2)}, u32[]{:S(2)}) async-start(bf16[128,8,896]{0,2,1:T(8,128)(2,1)} %bitcast.24), calls=%async_computation | async-start | bytes 3670016 | tf_op jit(solution)/shard_map/all_to_all | solution.py:49
  64.1 26.8 %all-to-all-done = bf16[128,8,896]{0,2,1:T(8,128)(2,1)S(1)} async-done(((bf16[128,8,896]{0,2,1:T(8,128)(2,1)}), bf16[128,8,896]{0,2,1:T(8,128)(2,1)S(1)}, u32[]{:S(2)}, u32[]{:S(2)}) %all-to-all-start) | async-done | bytes 1835040 | tf_op jit(solution)/shard_map/all_to_all | solution.py:49
  90.9 0.6 broadcast_in_dim.3
  91.5 25.4 %all-to-all-start.2 = ((s32[32,1,1]{2,1,0:T(1,128)}), s32[32,1,1]{2,1,0:T(1,128)S(1)}, u32[]{:S(2)}, u32[]{:S(2)}) async-start(s32[32,1,1]{2,1,0:T(1,128)} %broadcast_in_dim.3), calls=%async_computation.2 | async-start | bytes 32768 | tf_op jit(solution)/shard_map/all_to_all | solution.py:33
  116.9 2.6 copy.41
  119.5 1.8 all-gather.9.cloned.1.call-done
  121.3 2.7 copy.42
  123.9 0.1 copy-done
  124.0 1.1 copy-done.3
  125.1 5.7 %fusion = bf16[896,2048]{1,0:T(8,128)(2,1)} fusion(bf16[1024,896]{1,0:T(8,128)(2,1)S(1)} %bitcast.27, bf16[1024,2048]{1,0:T(8,128)(2,1)S(1)} %bitcast.26, bf16[1,896,2048]{2,1,0:T(8,128)(2,1)S(1)} %copy-done.3), kind=kOutput, calls=%fused_computation.2 | convolution fusion | flops 3765436416 | bytes 13369344 | tf_op jit(solution)/shard_map/dot_general | solution.py:42
  130.9 6.1 %copy.43 = bf16[896,2048]{0,1:T(8,128)(2,1)} copy(bf16[896,2048]{1,0:T(8,128)(2,1)} %fusion) | data formatting | bytes 7340032 | tf_op jit(solution)/shard_map/convert_element_type | solution.py:51
  136.9 0.0 all-to-all-done.2
  136.9 6.5 %all-to-all-start.1 = ((bf16[896,32,64]{0,2,1:T(8,128)(2,1)}), bf16[896,32,64]{0,2,1:T(8,128)(2,1)}, u32[]{:S(2)}, u32[]{:S(2)}) async-start(bf16[896,32,64]{0,2,1:T(8,128)(2,1)} %bitcast.21), calls=%async_computation.1 | async-start | bytes 7340032 | tf_op jit(solution)/shard_map/all_to_all | solution.py:54
  143.5 0.0 all-gather.7.cloned.1.call-start
  143.5 0.7 reduce_sum.9
  144.8 0.3 convert_reduce_fusion
  145.2 80.2 %all-to-all-done.1 = bf16[896,32,64]{0,2,1:T(8,128)(2,1)} async-done(((bf16[896,32,64]{0,2,1:T(8,128)(2,1)}), bf16[896,32,64]{0,2,1:T(8,128)(2,1)}, u32[]{:S(2)}, u32[]{:S(2)}) %all-to-all-start.1) | async-done | bytes 3670048 | tf_op jit(solution)/shard_map/all_to_all | solution.py:54
  225.4 7.8 %copy.44 = bf16[32,896,64]{2,1,0:T(8,128)(2,1)} copy(bf16[32,896,64]{1,2,0:T(8,128)(2,1)} %bitcast.9) | data formatting | bytes 7340032 | tf_op jit(solution)/shard_map/all_to_all | solution.py:54
  233.2 8.5 %reshape.37 = bf16[32,57344]{1,0:T(8,128)(2,1)} reshape(bf16[32,896,64]{2,1,0:T(8,128)(2,1)} %copy.44) | data formatting | bytes 7340032 | tf_op jit(solution)/shard_map/reshape | solution.py:56
  241.7 9.4 %dot_general.12 = bf16[896,64,32]{1,0,2:T(8,128)(2,1)} reshape(bf16[57344,32]{0,1:T(8,128)(2,1)} %bitcast.22) | data formatting | bytes 7340032 | tf_op jit(solution)/shard_map/dot_general | solution.py:58
  251.1 5.1 %multiply_reduce_fusion = f32[896,64]{1,0:T(8,128)S(1)} fusion(f32[32]{0:T(128)S(1)} %convert.2, bf16[896,64,32]{1,0,2:T(8,128)(2,1)} %dot_general.12), kind=kLoop, calls=%fused_computation | loop fusion | flops 5447680 | bytes 3899520
  256.2 0.2 copy.50
  256.4 0.9 add_convert_fusion
  257.3 0.0 all-gather.7.cloned.1.call-update
  257.3 62.3 %all-gather.7.cloned.1.call-done = bf16[896,2048]{0,1:T(8,128)(2,1)} async-done(((bf16[896,64]{0,1:T(8,128)(2,1)}), bf16[896,2048]{0,1:T(8,128)(2,1)}) %all-gather.7.cloned.1.call-update) | async-done | bytes 3670032 | tf_op jit(solution)/shard_map/all_gather | solution.py:66
  319.7 6.0 %copy.45 = bf16[896,2048]{1,0:T(8,128)(2,1)} copy(bf16[896,2048]{0,1:T(8,128)(2,1)} %all-gather.7.cloned.1.call-done) | data formatting | bytes 7340032
  (7 shorter events, 0.0 us)
Async XLA Ops:
  7.2 48.4 %all-gather.5.cloned.1.call-start = ((), (), s32[]{:S(2)}) async-start(), calls=%async_computation.3 | async-start | bytes 1572864 | tf_op jit(solution)/shard_map/all_gather | solution.py:20
  7.9 113.4 %all-gather.9.cloned.1.call-start = ((), (), s32[]{:S(2)}) async-start(), calls=%async_computation.5 | async-start | bytes 5242880 | tf_op jit(solution)/shard_map/all_gather | solution.py:20
  59.5 31.4 %all-to-all-start = ((bf16[128,8,896]{0,2,1:T(8,128)(2,1)}), bf16[128,8,896]{0,2,1:T(8,128)(2,1)S(1)}, u32[]{:S(2)}, u32[]{:S(2)}) async-start(bf16[128,8,896]{0,2,1:T(8,128)(2,1)} %bitcast.24), calls=%async_computation | async-start | bytes 3670016 | tf_op jit(solution)/shard_map/all_to_all | solution.py:49
  91.5 45.4 %all-to-all-start.2 = ((s32[32,1,1]{2,1,0:T(1,128)}), s32[32,1,1]{2,1,0:T(1,128)S(1)}, u32[]{:S(2)}, u32[]{:S(2)}) async-start(s32[32,1,1]{2,1,0:T(1,128)} %broadcast_in_dim.3), calls=%async_computation.2 | async-start | bytes 32768 | tf_op jit(solution)/shard_map/all_to_all | solution.py:33
  121.3 2.8 copy-start
  121.3 3.9 %copy-start.3 = (bf16[1,896,2048]{2,1,0:T(8,128)(2,1)S(1)}, bf16[1,896,2048]{2,1,0:T(8,128)(2,1)}, u32[]{:S(2)}) copy-start(bf16[1,896,2048]{2,1,0:T(8,128)(2,1)} %param.6) | copy-start | bytes 11010052
  136.9 88.5 %all-to-all-start.1 = ((bf16[896,32,64]{0,2,1:T(8,128)(2,1)}), bf16[896,32,64]{0,2,1:T(8,128)(2,1)}, u32[]{:S(2)}, u32[]{:S(2)}) async-start(bf16[896,32,64]{0,2,1:T(8,128)(2,1)} %bitcast.21), calls=%async_computation.1 | async-start | bytes 7340032 | tf_op jit(solution)/shard_map/all_to_all | solution.py:54
  143.5 176.2 %all-gather.7.cloned.1.call-start = ((), (), s32[]{:S(2)}) async-start(), calls=%async_computation.4 | async-start | bytes 3784704 | tf_op jit(solution)/shard_map/all_gather | solution.py:66
  251.1 5.3 %copy-start.1 = (f32[896,64]{0,1:T(8,128)S(1)}, f32[896,64]{0,1:T(8,128)}, u32[]{:S(2)}) copy-start(f32[896,64]{0,1:T(8,128)} %param.11) | copy-start | bytes 688132
  251.1 5.3 %copy-start.2 = (f32[896,64]{0,1:T(8,128)S(1)}, f32[896,64]{0,1:T(8,128)}, u32[]{:S(2)}) copy-start(f32[896,64]{0,1:T(8,128)} %param.10) | copy-start | bytes 688132
Sparse Core Ops, SparseCore 0:
  9.8 45.7 all-gather.4
  57.4 63.8 all-gather.8
  257.4 62.1 all-gather.6
where the time goes:
time: 333 us; the launch traced here: 332 us
  waiting for transfers between devices  219 us (66%)
  local copies, waits for them, and re-layouts  48.9 us (15%)
  starting transfers between devices  36 us (11%)
  between operations  15.1 us (5%)
  other arithmetic  7.03 us (2%)
  matrix products  5.74 us (2%)
    all_to_all x1, waiting for transfers between devices, local(): lax.all_to_all(inner, 'rep', split_axis=1, concat_axis=0, tiled=True)  80.2 us
    all_gather x1, waiting for transfers between devices, local(): new_y = lax.all_gather(block_y, 'rep', axis=1, tiled=True)  62.3 us
    all_gather x2, waiting for transfers between devices, all_blocks(): parts = lax.all_gather(parts, axes[k])  49.4 us
    all_to_all x1, waiting for transfers between devices, local(): lax.all_to_all(hidden_acts[0], FSDP, split_axis=1, concat_axis=0, tiled=T...  26.8 us
    all_to_all x1, starting transfers between devices, sent_to_all(): return lax.all_to_all(copies, axis, split_axis=0, concat_axis=0, tiled=True)  25.4 us
    unnamed x10, local copies, waits for them, and re-layouts  11.1 us
    dot_general x2, local copies, waits for them, and re-layouts, local(): jnp.dot(weights, stacked, preferred_element_type=jnp.float32)  9.55 us
    reshape x1, local copies, waits for them, and re-layouts, local(): stacked = blocks.reshape(replicas, rows * columns)  8.46 us
  transfers between devices with their start and end apart: 6, of which 5 were waited for; matrix products, arithmetic and copies ran while one was open for 7% of the time, Pallas kernels for 0%

commit v1 on v0

--- a/solution.py
+++ b/solution.py
@@ -6,6 +6,13 @@
 
 ROUND = 3
 FSDP = ("fsdp_0", "fsdp_1")
+
+
+def swapped_in(x, name, dim):
+    size = lax.axis_size(name)
+    blocks = jnp.stack([x for _ in range(size)])
+    blocks = lax.all_to_all(blocks, name, split_axis=0, concat_axis=0)
+    return jnp.concatenate(blocks, axis=dim)
 
 
 def in_order(parts, dim):
@@ -63,7 +70,7 @@
     mixing = 1.0 / (ROUND + 1.0)
     new_x = (1.0 - mixing) * outer_x + mixing * new_z
     block_y = (0.1 * new_z + 0.9 * new_x).astype(jnp.bfloat16)
-    new_y = lax.all_gather(block_y, "rep", axis=1, tiled=True)
+    new_y = swapped_in(block_y, "rep", 1)
     return (new_z, new_x, new_y)
 
 

time: 333 us -> 362 us (1.087)
  blocking collectives: 0 us -> 90.3 us
  waiting for transfers between devices: 219 us -> 157 us
    all_to_all x0 -> x1, blocking collectives: none -> 90.3 us  [swapped_in(): blocks = lax.all_to_all(blocks, name, split_axis=0, concat_axis=0)]
    all_gather x1 -> x0, waiting for transfers between devices: 62.3 us -> none  [local(): new_y = lax.all_gather(block_y, 'rep', axis=1, tiled=True)]
  transfers between devices with their start and end apart: 6 -> 5, of which waited for: 5 -> 4; matrix products, arithmetic and copies ran while one was open for 7% -> 6% of each run, Pallas kernels for 0% -> 0%
where the time goes in v1:
time: 362 us; the launch traced here: 361 us
  waiting for transfers between devices  157 us (43%)
  blocking collectives  90.3 us (25%)
  local copies, waits for them, and re-layouts  49.5 us (14%)
  starting transfers between devices  35.9 us (10%)
  between operations  15.4 us (4%)
  other arithmetic  7.02 us (2%)
  matrix products  5.74 us (2%)
    all_to_all x1, blocking collectives, swapped_in(): blocks = lax.all_to_all(blocks, name, split_axis=0, concat_axis=0)  90.3 us
    all_to_all x1, waiting for transfers between devices, local(): lax.all_to_all(inner, 'rep', split_axis=1, concat_axis=0, tiled=True)  80.3 us
    all_gather x2, waiting for transfers between devices, all_blocks(): parts = lax.all_gather(parts, axes[k])  49.4 us
    all_to_all x1, waiting for transfers between devices, local(): lax.all_to_all(hidden_acts[0], FSDP, split_axis=1, concat_axis=0, tiled=T...  26.8 us
    all_to_all x1, starting transfers between devices, sent_to_all(): return lax.all_to_all(copies, axis, split_axis=0, concat_axis=0, tiled=True)  25.4 us
    unnamed x10, local copies, waits for them, and re-layouts  11.1 us
    dot_general x2, local copies, waits for them, and re-layouts, local(): jnp.dot(weights, stacked, preferred_element_type=jnp.float32)  9.57 us
    reshape x1, local copies, waits for them, and re-layouts, local(): stacked = blocks.reshape(replicas, rows * columns)  8.46 us
  transfers between devices with their start and end apart: 5, of which 4 were waited for; matrix products, arithmetic and copies ran while one was open for 6% of the time, Pallas kernels for 0%

profile of v1, /device:TPU:1, one launch (start us, length us, event | category | flops | bytes accessed | tf_op | source)
XLA Modules:
  0.0 361.0 jit_solution(7514978546248207988)
XLA Ops:
  7.2 0.0 all-gather.4.cloned.1.call-start
  7.2 0.7 all-gather.4.cloned.1.call-update
  7.9 0.0 all-gather.6.cloned.1.call-start
  7.9 47.6 %all-gather.4.cloned.1.call-done = bf16[2,128,2048]{2,1,0:T(8,128)(2,1)} async-done(((bf16[1,128,2048]{2,1,0:T(8,128)(2,1)}), bf16[2,128,2048]{2,1,0:T(8,128)(2,1)}) %all-gather.4.cloned.1.call-update) | async-done | bytes 1048592 | tf_op jit(solution)/shard_map/all_gather | solution.py:27
  55.6 0.0 all-gather.6.cloned.1.call-update
  55.6 3.9 %copy.25 = bf16[1,128,7168]{1,2,0:T(8,128)(2,1)} copy(bf16[1,128,7168]{2,1,0:T(8,128)(2,1)} %param.7) | data formatting | bytes 3670016 | tf_op args[1]
  59.5 4.0 %all-to-all-start = ((bf16[128,8,896]{0,2,1:T(8,128)(2,1)}), bf16[128,8,896]{0,2,1:T(8,128)(2,1)S(1)}, u32[]{:S(2)}, u32[]{:S(2)}) async-start(bf16[128,8,896]{0,2,1:T(8,128)(2,1)} %bitcast.28), calls=%async_computation | async-start | bytes 3670016 | tf_op jit(solution)/shard_map/all_to_all | solution.py:56
  64.1 26.8 %all-to-all-done = bf16[128,8,896]{0,2,1:T(8,128)(2,1)S(1)} async-done(((bf16[128,8,896]{0,2,1:T(8,128)(2,1)}), bf16[128,8,896]{0,2,1:T(8,128)(2,1)S(1)}, u32[]{:S(2)}, u32[]{:S(2)}) %all-to-all-start) | async-done | bytes 1835040 | tf_op jit(solution)/shard_map/all_to_all | solution.py:56
  90.9 0.6 broadcast_in_dim.3
  91.5 25.4 %all-to-all-start.2 = ((s32[32,1,1]{2,1,0:T(1,128)}), s32[32,1,1]{2,1,0:T(1,128)S(1)}, u32[]{:S(2)}, u32[]{:S(2)}) async-start(s32[32,1,1]{2,1,0:T(1,128)} %broadcast_in_dim.3), calls=%async_computation.2 | async-start | bytes 32768 | tf_op jit(solution)/shard_map/all_to_all | solution.py:40
  116.9 2.6 copy.26
  119.5 1.8 all-gather.6.cloned.1.call-done
  121.3 2.7 copy.27
  123.9 0.1 copy-done
  124.0 1.1 copy-done.3
  125.1 5.7 %fusion = bf16[896,2048]{1,0:T(8,128)(2,1)} fusion(bf16[1024,896]{1,0:T(8,128)(2,1)S(1)} %bitcast.31, bf16[1024,2048]{1,0:T(8,128)(2,1)S(1)} %bitcast.30, bf16[1,896,2048]{2,1,0:T(8,128)(2,1)S(1)} %copy-done.3), kind=kOutput, calls=%fused_computation.2 | convolution fusion | flops 3765436416 | bytes 13369344 | tf_op jit(solution)/shard_map/dot_general | solution.py:49
  130.9 6.1 %copy.28 = bf16[896,2048]{0,1:T(8,128)(2,1)} copy(bf16[896,2048]{1,0:T(8,128)(2,1)} %fusion) | data formatting | bytes 7340032 | tf_op jit(solution)/shard_map/convert_element_type | solution.py:58
  136.9 0.0 all-to-all-done.2
  136.9 6.5 %all-to-all-start.1 = ((bf16[896,32,64]{0,2,1:T(8,128)(2,1)}), bf16[896,32,64]{0,2,1:T(8,128)(2,1)}, u32[]{:S(2)}, u32[]{:S(2)}) async-start(bf16[896,32,64]{0,2,1:T(8,128)(2,1)} %bitcast.24), calls=%async_computation.1 | async-start | bytes 7340032 | tf_op jit(solution)/shard_map/all_to_all | solution.py:61
  143.5 0.7 reduce_sum.9
  144.8 0.3 convert_reduce_fusion
  145.1 80.3 %all-to-all-done.1 = bf16[896,32,64]{0,2,1:T(8,128)(2,1)} async-done(((bf16[896,32,64]{0,2,1:T(8,128)(2,1)}), bf16[896,32,64]{0,2,1:T(8,128)(2,1)}, u32[]{:S(2)}, u32[]{:S(2)}) %all-to-all-start.1) | async-done | bytes 3670048 | tf_op jit(solution)/shard_map/all_to_all | solution.py:61
  225.4 7.8 %copy.29 = bf16[32,896,64]{2,1,0:T(8,128)(2,1)} copy(bf16[32,896,64]{1,2,0:T(8,128)(2,1)} %bitcast.9) | data formatting | bytes 7340032 | tf_op jit(solution)/shard_map/all_to_all | solution.py:61
  233.2 8.5 %reshape.45 = bf16[32,57344]{1,0:T(8,128)(2,1)} reshape(bf16[32,896,64]{2,1,0:T(8,128)(2,1)} %copy.29) | data formatting | bytes 7340032 | tf_op jit(solution)/shard_map/reshape | solution.py:63
  241.7 9.4 %dot_general.12 = bf16[896,64,32]{1,0,2:T(8,128)(2,1)} reshape(bf16[57344,32]{0,1:T(8,128)(2,1)} %bitcast.26) | data formatting | bytes 7340032 | tf_op jit(solution)/shard_map/dot_general | solution.py:65
  251.1 5.1 %multiply_reduce_fusion = f32[896,64]{1,0:T(8,128)S(1)} fusion(f32[32]{0:T(128)S(1)} %convert.2, bf16[896,64,32]{1,0,2:T(8,128)(2,1)} %dot_general.12), kind=kLoop, calls=%fused_computation | loop fusion | flops 5447680 | bytes 3899520
  256.3 0.2 copy.35
  256.4 0.0 copy-done.1
  256.4 0.9 add_convert_fusion
  257.3 0.5 stack.2
  257.8 90.3 %all_to_all.46 = bf16[32,896,64]{1,2,0:T(8,128)(2,1)} all-to-all(bf16[32,896,64]{1,2,0:T(8,128)(2,1)S(1)} %stack.2), channel_id=1, replica_groups=mesh['rep'=32,'fsdp_0'=2,'fsdp_1'=4] {'rep'}, dimensions={0} | all-to-all | bytes 7340032 | tf_op jit(solution)/shard_map/all_to_all | solution.py:14
  348.1 6.0 %copy.30 = bf16[896,2048]{1,0:T(8,128)(2,1)} copy(bf16[896,2048]{0,1:T(8,128)(2,1)} %bitcast.25) | data formatting | bytes 7340032
  (6 shorter events, 0.0 us)
Async XLA Ops:
  7.2 48.4 %all-gather.4.cloned.1.call-start = ((), (), s32[]{:S(2)}) async-start(), calls=%async_computation.4 | async-start | bytes 1572864 | tf_op jit(solution)/shard_map/all_gather | solution.py:27
  7.9 113.4 %all-gather.6.cloned.1.call-start = ((), (), s32[]{:S(2)}) async-start(), calls=%async_computation.5 | async-start | bytes 5242880 | tf_op jit(solution)/shard_map/all_gather | solution.py:27
  59.5 31.4 %all-to-all-start = ((bf16[128,8,896]{0,2,1:T(8,128)(2,1)}), bf16[128,8,896]{0,2,1:T(8,128)(2,1)S(1)}, u32[]{:S(2)}, u32[]{:S(2)}) async-start(bf16[128,8,896]{0,2,1:T(8,128)(2,1)} %bitcast.28), calls=%async_computation | async-start | bytes 3670016 | tf_op jit(solution)/shard_map/all_to_all | solution.py:56
  91.5 45.4 %all-to-all-start.2 = ((s32[32,1,1]{2,1,0:T(1,128)}), s32[32,1,1]{2,1,0:T(1,128)S(1)}, u32[]{:S(2)}, u32[]{:S(2)}) async-start(s32[32,1,1]{2,1,0:T(1,128)} %broadcast_in_dim.3), calls=%async_computation.2 | async-start | bytes 32768 | tf_op jit(solution)/shard_map/all_to_all | solution.py:40
  121.3 2.8 copy-start
  121.3 3.9 %copy-start.3 = (bf16[1,896,2048]{2,1,0:T(8,128)(2,1)S(1)}, bf16[1,896,2048]{2,1,0:T(8,128)(2,1)}, u32[]{:S(2)}) copy-start(bf16[1,896,2048]{2,1,0:T(8,128)(2,1)} %param.6) | copy-start | bytes 11010052
  136.9 88.5 %all-to-all-start.1 = ((bf16[896,32,64]{0,2,1:T(8,128)(2,1)}), bf16[896,32,64]{0,2,1:T(8,128)(2,1)}, u32[]{:S(2)}, u32[]{:S(2)}) async-start(bf16[896,32,64]{0,2,1:T(8,128)(2,1)} %bitcast.24), calls=%async_computation.1 | async-start | bytes 7340032 | tf_op jit(solution)/shard_map/all_to_all | solution.py:61
  251.1 5.3 %copy-start.1 = (f32[896,64]{0,1:T(8,128)S(1)}, f32[896,64]{0,1:T(8,128)}, u32[]{:S(2)}) copy-start(f32[896,64]{0,1:T(8,128)} %param.11) | copy-start | bytes 688132
  251.1 5.3 %copy-start.2 = (f32[896,64]{0,1:T(8,128)S(1)}, f32[896,64]{0,1:T(8,128)}, u32[]{:S(2)}) copy-start(f32[896,64]{0,1:T(8,128)} %param.10) | copy-start | bytes 688132
Sparse Core Ops, SparseCore 0:
  9.8 45.7 all-gather.3
  57.4 63.8 all-gather.5
